TPU v7x, 32 devices: a whole 2x2x4 slice. The times are simulated.
32 devices in a mesh: expert: 16 (over z, y, x), hidden: 2 (over core).
Axes of the slice: x: 2, y: 2, z: 4, core: 2. Of those that a mesh axis runs over, the one named last changes fastest.
Arguments:
- tokens: bfloat16 [1024, 4096], P('expert', 'hidden'), may hold values from -6 to 6
- route_ids: int32 [1024, 8], P('expert'), may hold values from 0 to 15, all different within a row; in each aligned block of 64 rows (0 to 63, 64 to 127, ...) at most 48 rows name the same one
- route_weights: float32 [1024, 8], P('expert'), may hold values from 0.05 to 1
- gate_up: bfloat16 [16, 2, 768, 4096], P('expert', None, 'hidden'), may hold values from -0.09375 to 0.09375
- down_proj: bfloat16 [16, 768, 4096], P('expert', None, 'hidden'), may hold values from -0.21875 to 0.21875
Outputs:
- layer_out: bfloat16 [1024, 4096], P('expert', 'hidden')
- hessian: float32 [16, 768, 768], P('expert', 'hidden')
Inputs may be any that keep to these rules, and one draw needn't show every extreme that they name: `route_ids`: each token names 8 different experts. Within the rows of one device (aligned blocks of 64 tokens) no expert is named more than 48 times, and in some block one expert is named exactly 48 times. Every expert is named by some token.
All inputs are finite; a program needn't handle non-finite values.
Results may differ from a plain program's by a relative error of at most 0.012.
Values may be sent and summed in bfloat16 or wider, within the bound.
A program may use at most 64 MiB of HBM per device.

v0:
```python
import jax
import jax.numpy as jnp
from jax import lax
from jax.sharding import PartitionSpec as P


def body(tokens, route_ids, route_weights, gate_up, down_proj):
    token_count = tokens.shape[0]
    route_top = route_ids.shape[1]
    local_experts = gate_up.shape[0]
    expert_devices = lax.axis_size("expert")
    all_experts = local_experts * expert_devices
    capacity = 3 * token_count * route_top // (2 * all_experts)
    flat_ids = route_ids.reshape(-1)
    route_total = flat_ids.shape[0]
    onehot = (flat_ids[:, None] == jnp.arange(all_experts, dtype=jnp.int32)[None, :]).astype(
        jnp.int32
    )
    earlier = jnp.cumsum(onehot, axis=0) - onehot
    slot_of = jnp.sum(earlier * onehot, axis=1)
    per_expert = jnp.sum(onehot, axis=0)
    target = flat_ids * capacity + slot_of
    matches = target[None, :] == jnp.arange(all_experts * capacity, dtype=jnp.int32)[:, None]
    filled = jnp.any(matches, axis=1)
    route_token = jnp.arange(route_total, dtype=jnp.int32)[None, :] // route_top
    source_row = jnp.sum(jnp.where(matches, route_token, 0), axis=1)
    sent_counts = per_expert.astype(jnp.bfloat16).reshape(all_experts, 1)
    zero_value = jnp.zeros((), jnp.bfloat16)
    features = lax.all_gather(tokens, "hidden", axis=1, tiled=True)
    outgoing = jnp.where(filled[:, None], features[source_row], zero_value).reshape(
        all_experts, capacity, features.shape[1]
    )
    arrived, arrived_counts = (
        lax.all_to_all(outgoing, "expert", split_axis=0, concat_axis=1, tiled=True),
        lax.all_to_all(sent_counts, "expert", split_axis=0, concat_axis=1, tiled=True),
    )
    projected = jnp.einsum("erd,egfd->ergf", arrived, gate_up, preferred_element_type=jnp.float32)
    hidden = (jax.nn.silu(projected[:, :, 0]) * projected[:, :, 1]).astype(jnp.bfloat16)
    part_rows = lax.all_gather(hidden, "hidden", axis=2, tiled=True)
    columns = jnp.einsum("erf,erg->efg", hidden, part_rows, preferred_element_type=jnp.float32)
    out_part = jnp.einsum("erg,egd->erd", part_rows, down_proj, preferred_element_type=jnp.float32)
    routed = jnp.sum(arrived_counts.astype(jnp.float32), axis=1)
    hessian = columns * (2.0 / routed)[:, None, None]
    returned = lax.all_to_all(
        out_part.astype(jnp.bfloat16), "expert", split_axis=1, concat_axis=0, tiled=True
    )
    feature_dev = returned.shape[2]
    picked = returned.reshape(all_experts * capacity, feature_dev)[target].reshape(
        token_count, route_top, feature_dev
    )
    route_share = route_weights / jnp.sum(route_weights, axis=1, keepdims=True)
    layer_out = jnp.einsum("tk,tkd->td", route_share, picked.astype(jnp.float32))
    return (layer_out.astype(jnp.bfloat16), hessian)


def solution(mesh):
    return jax.shard_map(
        body,
        mesh=mesh,
        in_specs=(
            P("expert", "hidden"),
            P("expert", None),
            P("expert", None),
            P("expert", None, "hidden", None),
            P("expert", None, "hidden"),
        ),
        out_specs=(P("expert", "hidden"), P("expert", "hidden", None)),
        check_vma=False,
    )
```

profile of v0, /device:TPU:8, one launch (start us, length us, event | category | flops | bytes accessed | tf_op | source)
XLA Modules:
  0.0 354.6 jit_solution(1843195980733694828)
XLA Ops:
  7.2 0.9 copy.23
  8.4 1.2 reduce-window.6
  9.5 0.2 slice_reduce_fusion
  9.8 0.2 convert_reduce_fusion
  9.9 0.2 fusion.11
  10.2 0.2 select_reduce_fusion
  10.4 3.8 %all_gather.6 = bf16[64,4096]{1,0:T(8,128)(2,1)} all-gather(bf16[64,2048]{1,0:T(8,128)(2,1)} %param.5), channel_id=1, replica_groups=mesh['expert'=16,'hidden'=2] {'hidden'}, dimensions={1}, use_global_device_ids=true | all-gather | bytes 786432 | tf_op jit(solution)/shard_map/all_gather | solution.py:29
  14.3 13.1 %gather_fusion = bf16[768,4096]{1,0:T(8,128)(2,1)} fusion(bf16[64,4096]{1,0:T(8,128)(2,1)} %all_gather.6, s32[1024]{0:T(1024)S(1)} %pad_clamp_fusion.1), kind=kCustom, calls=%fused_computation | custom fusion | bytes 12585984 | tf_op jit(solution)/shard_map/gather | solution.py:30
  27.4 3.3 broadcast_select_fusion
  30.7 145.9 %all_to_all.13 = bf16[16,48,4096]{2,1,0:T(8,128)(2,1)S(1)} all-to-all(bf16[16,48,4096]{2,1,0:T(8,128)(2,1)S(1)} %broadcast_select_fusion), channel_id=1, replica_groups=mesh['expert'=16,'hidden'=2] {'expert'}, dimensions={0} | all-to-all | bytes 12582912 | tf_op jit(solution)/shard_map/all_to_all | solution.py:34
  176.6 5.1 %fusion.8 = f32[1,768,2,384]{3,1,2,0:T(8,128)S(1)} fusion(bf16[768,4096,1]{1,0,2:T(8,128)(2,1)S(1)} %bitcast.81, bf16[1,2,384,4096]{3,2,1,0:T(8,128)(2,1)S(1)} %copy-done.4), kind=kOutput, calls=%fused_computation.11 | convolution fusion | flops 4831838208 | bytes 14942208 | tf_op jit(solution)/shard_map/erd,egfd->ergf/dot_general | solution.py:37
  181.7 1.4 copy-done.1
  183.1 1.2 fusion.15
  184.3 0.7 copy.28
  185.0 4.6 %all-to-all-start.2 = ((bf16[16,1,1]{2,1,0:T(2,128)(2,1)}), bf16[16,1,1]{2,1,0:T(2,128)(2,1)S(1)}, u32[]{:S(2)}, u32[]{:S(2)}) async-start(bf16[16,1,1]{2,1,0:T(2,128)(2,1)} %copy.28), calls=%async_computation.2 | async-start | bytes 16384 | tf_op jit(solution)/shard_map/all_to_all | solution.py:35
  189.5 2.8 all-gather.2.cloned.1.call-done
  192.4 4.1 %fusion.3 = bf16[1,768,2048]{2,1,0:T(8,128)(2,1)S(1)} fusion(bf16[1,768,2048]{2,1,0:T(8,128)(2,1)S(1)} %copy-done, bf16[1,768,768]{2,1,0:T(8,128)(2,1)} %all-gather.2.cloned.1.call-done), kind=kOutput, calls=%fused_computation.8 | convolution fusion | flops 2417491968 | bytes 7471104 | tf_op jit(solution)/shard_map/erg,egd->erd/dot_general | solution.py:41
  196.5 18.6 %copy.39 = bf16[1,768,2048]{2,0,1:T(2,128)(2,1)} copy(bf16[1,768,2048]{2,1,0:T(8,128)(2,1)S(1)} %fusion.3) | data formatting | bytes 6291456 | tf_op jit(solution)/shard_map/convert_element_type | solution.py:45
  215.0 0.5 broadcast.135
  215.6 20.6 %reduce.6 = bf16[768,2048]{1,0:T(8,128)(2,1)} reduce(bf16[768,1,2048]{2,1,0:T(2,128)(2,1)} %bitcast.79, bf16[]{:T(256)} %broadcast.135), dimensions={1}, to_apply=%bitcast.76.reduce_sub_computation | reduce | bytes 6291458
  236.1 7.0 %reshape.273 = bf16[16,2,49152]{2,1,0:T(2,128)(2,1)} reshape(bf16[768,2048]{1,0:T(8,128)(2,1)} %reduce.6) | data formatting | bytes 6291456
  243.2 7.1 %all-to-all-start.1 = ((bf16[16,2,49152]{2,1,0:T(2,128)(2,1)}), bf16[16,2,49152]{2,1,0:T(2,128)(2,1)}, u32[]{:S(2)}, u32[]{:S(2)}) async-start(bf16[16,2,49152]{2,1,0:T(2,128)(2,1)} %reshape.273), calls=%async_computation.1 | async-start | bytes 6291456 | tf_op jit(solution)/shard_map/all_to_all | solution.py:44
  250.4 0.1 mul.76
  250.5 0.1 copy.29
  250.7 0.6 convert_reduce_fusion.1
  252.0 3.7 %fusion.12 = f32[1,384,768]{2,1,0:T(8,128)} fusion(bf16[1,768,768]{2,1,0:T(8,128)(2,1)} %all-gather.2.cloned.1.call-done, f32[]{:T(128)S(6)} %div.42, f32[1,768,2,384]{3,1,2,0:T(8,128)} %copy-done.1), kind=kOutput, calls=%fused_computation.16 | convolution fusion | flops 455049216 | bytes 4718596 | tf_op jit(solution)/shard_map/erf,erg->efg/dot_general | solution.py:40
  255.7 63.4 %all-to-all-done.1 = bf16[16,2,49152]{2,1,0:T(2,128)(2,1)} async-done(((bf16[16,2,49152]{2,1,0:T(2,128)(2,1)}), bf16[16,2,49152]{2,1,0:T(2,128)(2,1)}, u32[]{:S(2)}, u32[]{:S(2)}) %all-to-all-start.1) | async-done | bytes 3145760 | tf_op jit(solution)/shard_map/all_to_all | solution.py:44
  319.2 11.5 %reshape.274 = bf16[768,1,2048]{2,1,0:T(2,128)(2,1)} reshape(bf16[16,2,49152]{2,1,0:T(2,128)(2,1)} %all-to-all-done.1) | data formatting | bytes 6291456
  330.6 6.4 %copy.37 = bf16[1,768,2048]{2,1,0:T(8,128)(2,1)} copy(bf16[1,768,2048]{2,0,1:T(2,128)(2,1)} %bitcast.80) | data formatting | bytes 6291456
  337.1 7.6 %gather_fusion.1 = bf16[512,2048]{1,0:T(8,128)(2,1)} fusion(bf16[768,2048]{1,0:T(8,128)(2,1)} %bitcast.77, s32[1024]{0:T(1024)S(1)} %pad_clamp_fusion), kind=kCustom, calls=%fused_computation.1 | custom fusion | bytes 4196352 | tf_op jit(solution)/shard_map/gather | solution.py:48
  344.7 2.3 fusion.6
  346.9 0.9 copy.38
  (29 shorter events, 0.6 us)
Async XLA Ops:
  7.2 185.2 %copy-start = (bf16[1,768,2048]{2,1,0:T(8,128)(2,1)S(1)}, bf16[1,768,2048]{2,1,0:T(8,128)(2,1)}, u32[]{:S(2)}) copy-start(bf16[1,768,2048]{2,1,0:T(8,128)(2,1)} %param.9) | copy-start | bytes 9437188
  7.2 185.2 %all-gather.2.cloned.1.call-start = ((), (), s32[]{:S(2)}) async-start(), calls=%async_computation.3 | async-start | bytes 1769472 | tf_op jit(solution)/shard_map/all_gather | solution.py:39
  30.7 145.9 %copy-start.4 = (bf16[1,2,384,4096]{3,2,1,0:T(8,128)(2,1)S(1)}, bf16[1,2,384,4096]{3,2,1,0:T(8,128)(2,1)}, u32[]{:S(2)}) copy-start(bf16[1,2,384,4096]{3,2,1,0:T(8,128)(2,1)} %param.8) | copy-start | bytes 18874372
  181.7 1.4 copy-start.1
  185.0 58.2 %all-to-all-start.2 = ((bf16[16,1,1]{2,1,0:T(2,128)(2,1)}), bf16[16,1,1]{2,1,0:T(2,128)(2,1)S(1)}, u32[]{:S(2)}, u32[]{:S(2)}) async-start(bf16[16,1,1]{2,1,0:T(2,128)(2,1)} %copy.28), calls=%async_computation.2 | async-start | bytes 16384 | tf_op jit(solution)/shard_map/all_to_all | solution.py:35
  243.2 7.1 %copy-start.2 = (s32[64,8]{0,1:T(8,128)S(1)}, s32[64,8]{0,1:T(8,128)}, u32[]{:S(2)}) copy-start(s32[64,8]{0,1:T(8,128)} %param.6) | copy-start | bytes 6148
  243.2 7.3 %copy-start.3 = (f32[64,8]{0,1:T(8,128)S(1)}, f32[64,8]{0,1:T(8,128)}, u32[]{:S(2)}) copy-start(f32[64,8]{0,1:T(8,128)} %param.7) | copy-start | bytes 6148
  243.2 76.0 %all-to-all-start.1 = ((bf16[16,2,49152]{2,1,0:T(2,128)(2,1)}), bf16[16,2,49152]{2,1,0:T(2,128)(2,1)}, u32[]{:S(2)}, u32[]{:S(2)}) async-start(bf16[16,2,49152]{2,1,0:T(2,128)(2,1)} %reshape.273), calls=%async_computation.1 | async-start | bytes 6291456 | tf_op jit(solution)/shard_map/all_to_all | solution.py:44
Sparse Core Ops, SparseCore 0:
  184.4 7.9 all-gather.1
where the time goes:
time: 359 us; the launch traced here: 355 us
  blocking collectives  150 us (42%)
  local copies, waits for them, and re-layouts  69.4 us (19%)
  waiting for transfers between devices  66.3 us (18%)
  other arithmetic  27.5 us (8%)
  matrix products  15.2 us (4%)
  between operations  14.9 us (4%)
  starting transfers between devices  11.7 us (3%)
    all_to_all x1, blocking collectives, body(): lax.all_to_all(outgoing, 'expert', split_axis=0, concat_axis=1, tiled=True)  146 us
    all_to_all x1, waiting for transfers between devices, body(): lax.all_to_all(out_part.astype(jnp.bfloat16), 'expert', split_axis=1, con...  63.4 us
    unnamed x15, local copies, waits for them, and re-layouts  27.8 us
    unnamed x1, other arithmetic  20.6 us
    convert_element_type x1, local copies, waits for them, and re-layouts, body(): out_part.astype(jnp.bfloat16)  18.6 us
    gather x1, local copies, waits for them, and re-layouts, body(): features[source_row]  13.1 us
    gather x1, local copies, waits for them, and re-layouts, body(): returned.reshape(all_experts * capacity, feature_dev)[target]  7.58 us
  transfers between devices with their start and end apart: 3, of which 2 were waited for; matrix products, arithmetic and copies ran while one was open for 16% of the time, Pallas kernels for 0%

commit v1 on v0

v1 whole, which is shorter than its diff:
```python
import jax
import jax.numpy as jnp
from jax import lax
from jax.sharding import PartitionSpec as P


def body(tokens, route_ids, route_weights, gate_up, down_proj):
    local_experts = gate_up.shape[0]
    all_experts = local_experts * lax.axis_size("expert")
    share = route_weights / jnp.sum(route_weights, axis=1, keepdims=True)
    hit = route_ids[:, :, None] == jnp.arange(all_experts, dtype=jnp.int32)[None, None, :]
    table = jnp.sum(jnp.where(hit, share[:, :, None], 0.0), axis=1)
    table = lax.all_gather(table.T, "expert", axis=1, tiled=True)
    mine = lax.dynamic_slice_in_dim(
        table, lax.axis_index("expert") * local_experts, local_experts, axis=0
    )
    features = lax.all_gather(tokens, "expert", axis=0, tiled=True)
    features = lax.all_gather(features, "hidden", axis=1, tiled=True)
    routed = jnp.sum((mine > 0).astype(jnp.float32), axis=1)
    gate = jnp.einsum("td,efd->etf", features, gate_up[:, 0], preferred_element_type=jnp.float32)
    upward = jnp.einsum("td,efd->etf", features, gate_up[:, 1], preferred_element_type=jnp.float32)
    hidden = jnp.where((mine > 0)[:, :, None], jax.nn.silu(gate) * upward, 0.0).astype(jnp.bfloat16)
    rows = lax.all_gather(hidden, "hidden", axis=2, tiled=True)
    columns = jnp.einsum("etf,etg->efg", hidden, rows, preferred_element_type=jnp.float32)
    hessian = columns * (2.0 / routed)[:, None, None]
    out = jnp.einsum("etg,egd->etd", rows, down_proj, preferred_element_type=jnp.float32)
    out = jnp.sum(out * mine[:, :, None], axis=0).astype(jnp.bfloat16)
    layer_out = lax.psum_scatter(out, "expert", scatter_dimension=0, tiled=True)
    return (layer_out, hessian)


def solution(mesh):
    return jax.shard_map(
        body,
        mesh=mesh,
        in_specs=(
            P("expert", "hidden"),
            P("expert", None),
            P("expert", None),
            P("expert", None, "hidden", None),
            P("expert", None, "hidden"),
        ),
        out_specs=(P("expert", "hidden"), P("expert", "hidden", None)),
        check_vma=False,
    )
```

time: 359 us -> 259 us (0.72)
  blocking collectives: 150 us -> 32.7 us
  waiting for transfers between devices: 66.3 us -> 183 us
  local copies, waits for them, and re-layouts: 69.4 us -> 0.16 us
  other arithmetic: 27.5 us -> 0.68 us
  starting transfers between devices: 11.7 us -> 0.16 us
  matrix products: 15.2 us -> 23.4 us
    all_to_all x1 -> x0, blocking collectives: 146 us -> none  [body(): lax.all_to_all(outgoing, 'expert', split_axis=0, concat_axis=1, tiled=True)]
    reduce_scatter x0 -> x1, waiting for transfers between devices: none -> 90.1 us  [body(): layer_out = lax.psum_scatter(out, 'expert', scatter_dimension=0, tiled=True)]
    all_gather x1 -> x3, waiting for transfers between devices: 2.83 us -> 92.4 us  [the longest x1 80.1 us: body(): features = lax.all_gather(tokens, 'expert', axis=0, tiled=True)]
    all_to_all x2 -> x0, waiting for transfers between devices: 63.4 us -> none  [the longest x1 63.4 us: body(): lax.all_to_all(out_part.astype(jnp.bfloat16), 'expert', split_axis=1, con...]
    all_gather x1, blocking collectives: 3.82 us -> 32.7 us  [body(): table = lax.all_gather(table.T, 'expert', axis=1, tiled=True)]
    unnamed x15 -> x9, local copies, waits for them, and re-layouts: 27.8 us -> 0.12 us
    gather x2 -> x0, local copies, waits for them, and re-layouts: 20.7 us -> none  [the longest x1 13.1 us: body(): features[source_row]]
    unnamed x1 -> x0, other arithmetic: 20.6 us -> none
  transfers between devices with their start and end apart: 3 -> 4, of which waited for: 2 -> 3; matrix products, arithmetic and copies ran while one was open for 16% -> 2% of each run, Pallas kernels for 0% -> 0%
where the time goes in v1:
time: 259 us; the launch traced here: 255 us
  waiting for transfers between devices  183 us (71%)
  blocking collectives  32.7 us (13%)
  matrix products  23.4 us (9%)
  between operations  14.5 us (6%)
    reduce_scatter x1, waiting for transfers between devices, body(): layer_out = lax.psum_scatter(out, 'expert', scatter_dimension=0, tiled=True)  90.1 us
    all_gather x1, waiting for transfers between devices, body(): features = lax.all_gather(tokens, 'expert', axis=0, tiled=True)  80.1 us
    all_gather x1, blocking collectives, body(): table = lax.all_gather(table.T, 'expert', axis=1, tiled=True)  32.7 us
    all_gather x1, waiting for transfers between devices, body(): rows = lax.all_gather(hidden, 'hidden', axis=2, tiled=True)  12.3 us
    dot_general x1, matrix products, body(): jnp.einsum('td,efd->etf', features, gate_up[:, 0], preferred_element_type...  6.99 us
    dot_general x1, matrix products, body(): jnp.einsum('etg,egd->etd', rows, down_proj, preferred_element_type=jnp.fl...  6.45 us
    dot_general x1, matrix products, body(): jnp.einsum('td,efd->etf', features, gate_up[:, 1], preferred_element_type...  6.45 us
  transfers between devices with their start and end apart: 4, of which 3 were waited for; matrix products, arithmetic and copies ran while one was open for 2% of the time, Pallas kernels for 0%

profile of v1, /device:TPU:8, one launch (start us, length us, event | category | flops | bytes accessed | tf_op | source)
XLA Modules:
  0.0 254.8 jit_solution(13706966847959692181)
XLA Ops:
  7.2 0.0 copy-start
  7.2 0.0 copy-start.1
  7.2 0.0 copy-start.2
  7.2 0.0 all-gather.5.cloned.1.call-start
  7.2 0.7 all-gather.5.cloned.1.call-update
  7.9 0.0 all-gather.7.cloned.1.call-start
  8.0 80.1 %all-gather.5.cloned.1.call-done = bf16[1024,2048]{1,0:T(8,128)(2,1)} async-done(((bf16[64,2048]{1,0:T(8,128)(2,1)}), bf16[1024,2048]{1,0:T(8,128)(2,1)}) %all-gather.5.cloned.1.call-update) | async-done | bytes 4194320 | tf_op jit(solution)/shard_map/all_gather | solution.py:17
  88.1 0.0 all-gather.7.cloned.1.call-update
  88.1 0.0 all-gather.9.cloned.1.call-start
  88.2 0.0 copy-done.1
  88.2 0.0 copy-done.2
  88.2 32.7 %all-gather = f32[16,64,16]{1,2,0:T(8,128)S(1)} all-gather(f32[1,64,16]{1,2,0:T(8,128)S(1)} %bitcast.54), channel_id=1, replica_groups=mesh['expert'=16,'hidden'=2] {'expert'}, dimensions={0}, use_global_device_ids=true | all-gather | bytes 69632 | tf_op jit(solution)/shard_map/all_gather | solution.py:13
  121.0 0.1 reshape.52
  121.1 0.6 fusion.24
  121.7 0.0 all-gather.7.cloned.1.call-done
  121.7 0.0 copy-start.3
  121.7 7.0 %fusion.3 = f32[384,1024]{1,0:T(8,128)S(1)} fusion(bf16[1024,4096]{1,0:T(8,128)(2,1)} %all-gather.7.cloned.1.call-done, bf16[1,2,384,4096]{3,2,1,0:T(8,128)(2,1)} %param.8), kind=kOutput, calls=%fused_computation.4 | convolution fusion | flops 3221225472 | bytes 13107200 | tf_op jit(solution)/shard_map/td,efd->etf/dot_general | solution.py:20
  128.7 0.0 copy-done.3
  128.8 6.4 %fusion.8 = bf16[1,1024,384]{1,2,0:T(8,128)(2,1)} fusion(f32[384,1024]{1,0:T(8,128)S(1)} %fusion.3, bf16[1024,4096]{1,0:T(8,128)(2,1)S(1)} %copy-done.3, bf16[1,2,384,4096]{3,2,1,0:T(8,128)(2,1)} %param.8, pred[1024]{0:T(1024)(128)(4,1)S(1)} %compare_reduce_fusion), kind=kOutput, calls=%fused_computation.10 | convolution fusion | flops 3223977984 | bytes 13894656 | tf_op jit(solution)/shard_map/td,efd->etf/dot_general | solution.py:21
  135.2 0.0 all-gather.9.cloned.1.call-update
  135.2 0.0 reduce-scatter.2.cloned.1.call-start
  135.3 12.3 %all-gather.9.cloned.1.call-done = bf16[1,1024,768]{1,2,0:T(8,128)(2,1)} async-done(((bf16[1,1024,384]{1,2,0:T(8,128)(2,1)}), bf16[1,1024,768]{1,2,0:T(8,128)(2,1)}) %all-gather.9.cloned.1.call-update) | async-done | bytes 1572880 | tf_op jit(solution)/shard_map/all_gather | solution.py:23
  147.6 0.0 copy-done
  147.6 6.4 %multiply_convert_fusion = bf16[1024,2048]{1,0:T(8,128)(2,1)} fusion(f32[1024]{0:T(1024)S(1)} %bitcast.55, bf16[1,768,2048]{2,1,0:T(8,128)(2,1)S(1)} %copy-done, bf16[1,1024,768]{1,2,0:T(8,128)(2,1)} %all-gather.9.cloned.1.call-done), kind=kOutput, calls=%fused_computation | convolution fusion | flops 3225419776 | bytes 8916992 | tf_op jit(solution)/shard_map/etg,egd->etd/dot_general | solution.py:26
  154.0 0.0 reduce-scatter.2.cloned.1.call-update
  154.7 3.5 %fusion.20 = f32[1,384,768]{2,1,0:T(8,128)} fusion(bf16[1,1024,768]{1,2,0:T(8,128)(2,1)} %all-gather.9.cloned.1.call-done, bf16[1,1024,384]{1,2,0:T(8,128)(2,1)} %fusion.8, f32[]{:T(128)S(6)} %div.19), kind=kOutput, calls=%fused_computation.20 | convolution fusion | flops 604274688 | bytes 3538948 | tf_op jit(solution)/shard_map/etf,etg->efg/dot_general | solution.py:24
  158.2 90.1 %reduce-scatter.2.cloned.1.call-done = bf16[64,2048]{1,0:T(8,128)(2,1)} async-done(((bf16[1024,2048]{1,0:T(8,128)(2,1)}), bf16[64,2048]{1,0:T(8,128)(2,1)}) %reduce-scatter.2.cloned.1.call-update) | async-done | bytes 262160 | tf_op jit(solution)/shard_map/reduce_scatter | solution.py:28
  (5 shorter events, 0.1 us)
Async XLA Ops:
  7.2 140.4 %copy-start = (bf16[1,768,2048]{2,1,0:T(8,128)(2,1)S(1)}, bf16[1,768,2048]{2,1,0:T(8,128)(2,1)}, u32[]{:S(2)}) copy-start(bf16[1,768,2048]{2,1,0:T(8,128)(2,1)} %param.9) | copy-start | bytes 9437188
  7.2 81.0 %copy-start.1 = (f32[64,8]{0,1:T(8,128)S(1)}, f32[64,8]{0,1:T(8,128)}, u32[]{:S(2)}) copy-start(f32[64,8]{0,1:T(8,128)} %param.7) | copy-start | bytes 6148
  7.2 81.0 %copy-start.2 = (s32[64,8]{0,1:T(8,128)S(1)}, s32[64,8]{0,1:T(8,128)}, u32[]{:S(2)}) copy-start(s32[64,8]{0,1:T(8,128)} %param.6) | copy-start | bytes 6148
  7.2 80.9 %all-gather.5.cloned.1.call-start = ((), (), s32[]{:S(2)}) async-start(), calls=%async_computation.1 | async-start | bytes 4456448 | tf_op jit(solution)/shard_map/all_gather | solution.py:17
  7.9 113.8 %all-gather.7.cloned.1.call-start = ((), (), s32[]{:S(2)}) async-start(), calls=%async_computation.2 | async-start | bytes 12582912 | tf_op jit(solution)/shard_map/all_gather | solution.py:18
  88.1 59.5 %all-gather.9.cloned.1.call-start = ((), (), s32[]{:S(2)}) async-start(), calls=%async_computation.3 | async-start | bytes 2359296 | tf_op jit(solution)/shard_map/all_gather | solution.py:23
  121.7 7.0 %copy-start.3 = (bf16[1024,4096]{1,0:T(8,128)(2,1)S(1)}, bf16[1024,4096]{1,0:T(8,128)(2,1)}, u32[]{:S(2)}) copy-start(bf16[1024,4096]{1,0:T(8,128)(2,1)} %all-gather.7.cloned.1.call-done) | copy-start | bytes 25165828
  135.2 113.0 %reduce-scatter.2.cloned.1.call-start = ((), (), s32[]{:S(2)}) async-start(), calls=%async_computation.4 | async-start | bytes 4456448 | tf_op jit(solution)/shard_map/reduce_scatter | solution.py:28
Sparse Core Ops, SparseCore 0:
  10.8 77.2 all-gather.4
  89.6 18.7 all-gather.6
  135.3 12.1 all-gather.8
  154.2 94.0 reduce-scatter.1

commit v2 on v1

--- a/solution.py
+++ b/solution.py
@@ -1,7 +1,323 @@
 import jax
 import jax.numpy as jnp
 from jax import lax
+from jax.experimental import pallas as pl
+from jax.experimental.pallas import tpu as pltpu
 from jax.sharding import PartitionSpec as P
+
+PLANES = 4
+PLANE = 4
+FIRST = (1, 2, 1, 2)
+SECOND = (2, 0, 3, 1)
+THIRD = (3, 3, 0, 0)
+NAMES = ("zr", "xr", "yr", "dx", "dy", "c0", "c1", "c2", "c3", "tz", "tx", "ty", "td", "hr",
+         "ax", "ay", "bx0", "bx1", "by0", "by1", "z0", "z1")
+SENDS = 128
+
+
+def pick(values, z):
+    chosen = jnp.int32(values[0])
+    for place in range(1, len(values)):
+        chosen = jnp.where(z == place, jnp.int32(values[place]), chosen)
+    return chosen
+
+
+def layer_kernel(tokens, table, gate_up, down, out, hess,
+                 feats, shares, hid, part, got_ax, got_ay, got_bx, got_by, got_z,
+                 w_gate, w_down, send_sem, recv_sem, load_sem):
+    rows, width = tokens.shape
+    half = rows // 2
+    units = hid.shape[-1]
+    me = lax.axis_index("expert")
+    c = lax.axis_index("hidden")
+    z, j = me // PLANE, me % PLANE
+    xj, yj, dj = j + 1 - 2 * (j % 2), (j + 2) % PLANE, PLANE - 1 - j
+    ex, ey = z * PLANE + xj, z * PLANE + yj
+    at_end = z % (PLANES - 1) == 0
+    inside = z % (PLANES - 1) != 0
+    a1, a2, a3 = pick(FIRST, z), pick(SECOND, z), pick(THIRD, z)
+    order = (z, a1, a3, a2)
+    lo, hi = pl.ds(0, half), pl.ds(half, half)
+    all_rows = pl.ds(0, rows)
+    started = []
+
+    load_gate = pltpu.make_async_copy(gate_up.at[0], w_gate, load_sem.at[0])
+    load_down = pltpu.make_async_copy(down.at[0], w_down, load_sem.at[1])
+    load_gate.start()
+    load_down.start()
+
+    def sem(name, k):
+        return recv_sem.at[NAMES.index(name) * PLANES + k]
+
+    def send(src, dst, to, name, k, core=None, when=None):
+        copy = pltpu.make_async_remote_copy(
+            src_ref=src, dst_ref=dst, send_sem=send_sem.at[len(started)], recv_sem=sem(name, k),
+            device_id=(to, c if core is None else core), device_id_type=pl.DeviceIdType.MESH)
+        started.append((copy, when))
+        if when is None:
+            copy.start()
+        else:
+            pl.when(when)(copy.start)
+
+    def landed(dst, name, k):
+        pltpu.make_async_remote_copy(
+            src_ref=dst, dst_ref=dst, send_sem=send_sem.at[0], recv_sem=sem(name, k),
+            device_id=(me, 1 - c), device_id_type=pl.DeviceIdType.MESH).wait_recv()
+
+    def block(k, q, part_rows=all_rows):
+        return feats.at[c, k, q, part_rows]
+
+    def across(k, q, name):
+        send(block(k, q), block(k, q), me, name, k, core=1 - c)
+
+    def sides(k):
+        for to, name, tname in ((ex, "xr", "tx"), (ey, "yr", "ty")):
+            send(shares.at[k, j], shares.at[k, j], to, tname, k)
+            send(block(k, j), block(k, j), to, name, k)
+
+    def column(k):
+        landed(shares.at[k, j], "tz", k)
+        landed(block(k, j), "zr", k)
+        to = jnp.where(k < z, me + PLANE, me - PLANE)
+        send(shares.at[k, j], shares.at[k, j], to, "tz", k, when=inside)
+        send(block(k, j), block(k, j), to, "zr", k, when=inside)
+        across(k, j, "c0")
+
+    def relay(k):
+        landed(shares.at[k, yj], "ty", k)
+        landed(shares.at[k, xj], "tx", k)
+        send(shares.at[k, yj], shares.at[k, yj], ex, "td", k)
+        landed(block(k, yj), "yr", k)
+        send(block(k, yj, lo), block(k, yj, lo), ex, "dx", k)
+        across(k, yj, "c2")
+        landed(block(k, xj), "xr", k)
+        send(block(k, xj, hi), block(k, xj, hi), ey, "dy", k)
+        across(k, xj, "c1")
+
+    def corner(k):
+        landed(shares.at[k, dj], "td", k)
+        landed(block(k, dj, lo), "dx", k)
+        landed(block(k, dj, hi), "dy", k)
+        across(k, dj, "c3")
+
+    def other_core(k):
+        for q, name in ((j, "c0"), (xj, "c1"), (yj, "c2"), (dj, "c3")):
+            landed(feats.at[1 - c, k, q], name, k)
+
+    def my_share(k):
+        lanes = shares.shape[-1]
+        row, off = me * rows // lanes, me * rows % lanes
+        lane = lax.broadcasted_iota(jnp.int32, (rows, lanes), 1)
+        line = lax.broadcasted_iota(jnp.int32, (rows, lanes), 0)
+        columns = []
+        for q in range(PLANE):
+            values = jnp.broadcast_to(shares[k, q, pl.ds(row, 1), :], (rows, lanes))
+            columns.append(jnp.sum(jnp.where(lane == line + off, values, 0.0), axis=1, keepdims=True))
+        return jnp.concatenate(columns, axis=0)
+
+    def up_side(k, w):
+        total = None
+        for side in range(2):
+            x = feats[side, k].reshape(PLANE * rows, width)
+            wg = w_gate[:, :, side * width:(side + 1) * width].reshape(2 * units, width)
+            term = lax.dot_general(x, wg, (((1,), (1,)), ((), ())), preferred_element_type=jnp.float32)
+            total = term if total is None else total + term
+        gate, upward = total[:, :units], total[:, units:]
+        value = gate / (1.0 + jnp.exp(-gate)) * upward
+        hid[c, k] = jnp.where(w > 0, value, 0.0).astype(jnp.bfloat16)
+        send(hid.at[c, k], hid.at[c, k], me, "hr", k, core=1 - c)
+
+    def down_side(k, w, first):
+        landed(hid.at[1 - c, k], "hr", k)
+        mine = hid[c, k]
+        for side in range(2):
+            cols = slice(side * units, (side + 1) * units)
+            gram = lax.dot_general(mine, hid[side, k], (((0,), (0,)), ((), ())),
+                                   preferred_element_type=jnp.float32)
+            hess[0, :, cols] = gram if first else hess[0, :, cols] + gram
+        step = 512
+        for start in range(0, width, step):
+            cols = slice(start, start + step)
+            o = jnp.dot(hid[0, k], w_down[:units, cols], preferred_element_type=jnp.float32)
+            o = o + jnp.dot(hid[1, k], w_down[units:, cols], preferred_element_type=jnp.float32)
+            part[k, :, :, cols] = (o * w).astype(jnp.bfloat16).reshape(PLANE, rows, step)
+
+    def give(k):
+        send(part.at[k, dj, lo], got_ax.at[k], ex, "ax", k)
+        send(part.at[k, dj, hi], got_ay.at[k], ey, "ay", k)
+        send(part.at[k, xj, lo], got_bx.at[k, lo], ex, "bx0", k)
+        send(part.at[k, yj, hi], got_by.at[k, hi], ey, "by1", k)
+
+    def add_up(*terms):
+        total = terms[0].astype(jnp.float32)
+        for term in terms[1:]:
+            total = total + term.astype(jnp.float32)
+        return total.astype(jnp.bfloat16)
+
+    def pass_on(k):
+        landed(got_ax.at[k], "ax", k)
+        part[k, yj, lo] = add_up(part[k, yj, lo], got_ax[k])
+        send(part.at[k, yj, lo], got_by.at[k, lo], ey, "by0", k)
+        landed(got_ay.at[k], "ay", k)
+        part[k, xj, hi] = add_up(part[k, xj, hi], got_ay[k])
+        send(part.at[k, xj, hi], got_bx.at[k, hi], ex, "bx1", k)
+
+    def plane_done(k):
+        landed(got_bx.at[k, lo], "bx0", k)
+        landed(got_bx.at[k, hi], "bx1", k)
+        landed(got_by.at[k, lo], "by0", k)
+        landed(got_by.at[k, hi], "by1", k)
+
+    def z_sem(slot, k):
+        return recv_sem.at[(NAMES.index("z0") + slot) * PLANES + k]
+
+    def z_copy(k):
+        slot = jnp.where(k > z, 0, 1)
+        to = jnp.where(k > z, me + PLANE, me - PLANE)
+        copy = pltpu.make_async_remote_copy(
+            src_ref=part.at[k, j], dst_ref=got_z.at[slot, k], send_sem=send_sem.at[len(started)],
+            recv_sem=z_sem(slot, k), device_id=(to, c), device_id_type=pl.DeviceIdType.MESH)
+        return copy, slot
+
+    def chain_end(k):
+        copy, _ = z_copy(k)
+        started.append((copy, at_end))
+
+        @pl.when(at_end)
+        def _():
+            plane_done(k)
+            part[k, j] = add_up(part[k, j], got_bx[k], got_by[k])
+            copy.start()
+
+    def chain_inside(k):
+        copy, slot = z_copy(k)
+        started.append((copy, inside))
+
+        @pl.when(inside)
+        def _():
+            plane_done(k)
+            copy.wait_recv()
+            part[k, j] = add_up(part[k, j], got_bx[k], got_by[k], got_z[slot, k])
+            copy.start()
+
+    feats[c, z, j] = tokens[...]
+    shares[z, j] = table[...]
+    barrier = pltpu.get_barrier_semaphore()
+
+    def greet(to, core):
+        pl.semaphore_signal(barrier, inc=1, device_id=(to, core), device_id_type=pl.DeviceIdType.MESH)
+
+    greet(me, 1 - c)
+    greet(ex, c)
+    greet(ey, c)
+    pl.when(z > 0)(lambda: greet(me - PLANE, c))
+    pl.when(z < PLANES - 1)(lambda: greet(me + PLANE, c))
+    pl.when(at_end)(lambda: pl.semaphore_wait(barrier, 4))
+    pl.when(inside)(lambda: pl.semaphore_wait(barrier, 5))
+
+    for to, when in ((me - PLANE, z > 0), (me + PLANE, z < PLANES - 1)):
+        send(shares.at[z, j], shares.at[z, j], to, "tz", z, when=when)
+        send(block(z, j), block(z, j), to, "zr", z, when=when)
+    sides(z)
+    across(z, j, "c0")
+    column(a1)
+    sides(a1)
+    relay(order[0])
+    column(a2)
+    corner(order[0])
+    relay(order[1])
+    column(a3)
+    sides(a3)
+    sides(a2)
+
+    load_gate.wait()
+    load_down.wait()
+    count = None
+    for i, k in enumerate(order):
+        other_core(k)
+        w = my_share(k)
+        hits = jnp.sum((w > 0).astype(jnp.float32), axis=0, keepdims=True)
+        count = hits if count is None else count + hits
+        up_side(k, w)
+        if i + 2 < PLANES:
+            relay(order[i + 2])
+        down_side(k, w, i == 0)
+        give(k)
+        if i + 1 < PLANES:
+            corner(order[i + 1])
+        if i >= 1:
+            pass_on(order[i - 1])
+        if i >= 2:
+            chain_end(order[i - 1])
+    pass_on(order[3])
+    hess[0] = hess[0] * (2.0 / count)
+    chain_end(order[3])
+    chain_inside(a3)
+    chain_inside(pick((0, 0, 3, 0), z))
+    chain_inside(pick((0, 2, 1, 0), z))
+    plane_done(z)
+
+    @pl.when(at_end)
+    def _():
+        slot = jnp.where(z > 0, 0, 1)
+        pltpu.make_async_remote_copy(
+            src_ref=part.at[z, j], dst_ref=got_z.at[slot, z], send_sem=send_sem.at[0],
+            recv_sem=z_sem(slot, z), device_id=(me, 1 - c),
+            device_id_type=pl.DeviceIdType.MESH).wait_recv()
+        out[...] = add_up(part[z, j], got_bx[z], got_by[z], got_z[slot, z])
+
+    @pl.when(inside)
+    def _():
+        landed(got_z.at[0, z], "z0", z)
+        landed(got_z.at[1, z], "z1", z)
+        out[...] = add_up(part[z, j], got_bx[z], got_by[z], got_z[0, z], got_z[1, z])
+
+    for copy, when in started:
+        if when is None:
+            copy.wait_send()
+        else:
+            pl.when(when)(copy.wait_send)
+
+
+def kernel_body(tokens, route_ids, route_weights, gate_up, down_proj):
+    rows, width = tokens.shape
+    experts = lax.axis_size("expert")
+    units = gate_up.shape[2]
+    lanes = 128
+    share = route_weights / jnp.sum(route_weights, axis=1, keepdims=True)
+    hit = route_ids[None] == jnp.arange(experts, dtype=jnp.int32)[:, None, None]
+    table = jnp.sum(jnp.where(hit, share[None], 0.0), axis=2).reshape(experts * rows // lanes, lanes)
+    bf, f32 = jnp.bfloat16, jnp.float32
+    out, hess = pl.pallas_call(
+        layer_kernel,
+        out_shape=(
+            jax.ShapeDtypeStruct((rows, width), bf),
+            jax.ShapeDtypeStruct((1, units, 2 * units), f32),
+        ),
+        in_specs=[pl.BlockSpec(memory_space=pltpu.VMEM)] * 2 + [pl.BlockSpec(memory_space=pl.ANY)] * 2,
+        out_specs=(pl.BlockSpec(memory_space=pltpu.VMEM),) * 2,
+        scratch_shapes=[
+            pltpu.VMEM((2, PLANES, PLANE, rows, width), bf),
+            pltpu.VMEM((PLANES, PLANE) + table.shape, f32),
+            pltpu.VMEM((2, PLANES, PLANE * rows, units), bf),
+            pltpu.VMEM((PLANES, PLANE, rows, width), bf),
+            pltpu.VMEM((PLANES, rows // 2, width), bf),
+            pltpu.VMEM((PLANES, rows // 2, width), bf),
+            pltpu.VMEM((PLANES, rows, width), bf),
+            pltpu.VMEM((PLANES, rows, width), bf),
+            pltpu.VMEM((2, PLANES, rows, width), bf),
+            pltpu.VMEM(gate_up.shape[1:], bf),
+            pltpu.VMEM(down_proj.shape[1:], bf),
+            pltpu.SemaphoreType.DMA((SENDS,)),
+            pltpu.SemaphoreType.DMA((len(NAMES) * PLANES,)),
+            pltpu.SemaphoreType.DMA((2,)),
+        ],
+        compiler_params=pltpu.CompilerParams(
+            collective_id=0, has_side_effects=True, vmem_limit_bytes=56 * 1024 * 1024
+        ),
+        name="moe_layer",
+    )(tokens, table, gate_up, down_proj)
+    return (out, hess)
 
 
 def body(tokens, route_ids, route_weights, gate_up, down_proj):
@@ -30,8 +346,9 @@
 
 
 def solution(mesh):
+    in_plane = mesh.shape["expert"] == PLANES * PLANE and mesh.shape["hidden"] == 2
     return jax.shard_map(
-        body,
+        kernel_body if in_plane else body,
         mesh=mesh,
         in_specs=(
             P("expert", "hidden"),

time: 259 us -> 115 us (0.44); the launches traced: 255 us -> 114 us
  waiting for transfers between devices: 183 us -> 0 us
  Pallas kernels: 0 us -> 106 us
  blocking collectives: 32.7 us -> 0 us
  matrix products: 23.4 us -> 0 us
  between operations: 14.5 us -> 0.64 us
  local copies, waits for them, and re-layouts: 0.16 us -> 4.69 us
    pallas_call x0 -> x1, Pallas kernels: none -> 106 us  [kernel_body(): pl.pallas_call(layer_kernel, out_shape=(jax.ShapeDtypeStruct((rows, width...]
    all_gather x3 -> x0, waiting for transfers between devices: 92.4 us -> none  [the longest x1 80.1 us: body(): features = lax.all_gather(tokens, 'expert', axis=0, tiled=True)]
    reduce_scatter x1 -> x0, waiting for transfers between devices: 90.1 us -> none  [body(): layer_out = lax.psum_scatter(out, 'expert', scatter_dimension=0, tiled=True)]
    all_gather x1 -> x0, blocking collectives: 32.7 us -> none  [body(): table = lax.all_gather(table.T, 'expert', axis=1, tiled=True)]
    dot_general x4 -> x0, matrix products: 23.4 us -> none  [the longest x1 6.99 us: body(): jnp.einsum('td,efd->etf', features, gate_up[:, 0], preferred_element_type...]
    unnamed x9 -> x2, local copies, waits for them, and re-layouts: 0.12 us -> 4.03 us
  transfers between devices with their start and end apart: 4 -> 0, of which waited for: 3 -> 0; matrix products, arithmetic and copies ran while one was open for 2% -> 0% of each run, Pallas kernels for 0% -> 0%
where the time goes in v2:
time: 115 us; the launch traced here: 114 us
  Pallas kernels  106 us (92%)
  local copies, waits for them, and re-layouts  4.69 us (4%)
  other arithmetic  2.11 us (2%)
    pallas_call x1, Pallas kernels, kernel_body(): pl.pallas_call(layer_kernel, out_shape=(jax.ShapeDtypeStruct((rows, width...  106 us
    unnamed x2, local copies, waits for them, and re-layouts  4.03 us

profile of v2, /device:TPU:8, one launch (start us, length us, event | category | flops | bytes accessed | tf_op | source)
XLA Modules:
  0.0 113.5 jit_solution(15726030150543073417)
XLA Ops:
  0.6 0.7 reduce_sum.18
  1.3 0.7 broadcast_divide_fusion
  2.0 0.7 select_reduce_fusion
  2.7 0.7 reshape.10.table
  3.4 106.1 %moe_layer.1 = (bf16[64,2048]{1,0:T(8,128)(2,1)}, f32[1,384,768]{2,1,0:T(8,128)}) custom-call(bf16[64,2048]{1,0:T(8,128)(2,1)} %tokens.1, f32[8,128]{1,0:T(8,128)} %reshape.10.table, bf16[1,2,384,4096]{3,2,1,0:T(8,128)(2,1)} %gate_up.1, bf16[1,768,2048]{2,1,0:T(8,128)(2,1)} %down.1), custom_call_target="tpu_custom_call" | custom-call | tf_op jit(solution)/shard_map/moe_layer/pallas_call | solution.py:291
  109.5 1.7 %copy.11 = bf16[64,2048]{1,0:T(8,128)(2,1)} copy(bf16[64,2048]{1,0:T(8,128)(2,1)} %get-tuple-element.4) | data formatting | bytes 524288
  111.1 2.4 %copy.12 = f32[1,384,768]{2,1,0:T(8,128)} copy(f32[1,384,768]{2,1,0:T(8,128)} %get-tuple-element.5) | data formatting | bytes 2359296

commit v3 on v2

--- a/solution.py
+++ b/solution.py
@@ -11,7 +11,7 @@
 SECOND = (2, 0, 3, 1)
 THIRD = (3, 3, 0, 0)
 NAMES = ("zr", "xr", "yr", "dx", "dy", "c0", "c1", "c2", "c3", "tz", "tx", "ty", "td", "hr",
-         "ax", "ay", "bx0", "bx1", "by0", "by1", "z0", "z1")
+         "ax", "ay", "bx0", "bx1", "by0", "by1", "z00", "z01", "z10", "z11")
 SENDS = 128
 
 
@@ -22,7 +22,7 @@
     return chosen
 
 
-def layer_kernel(tokens, table, gate_up, down, out, hess,
+def layer_kernel(tokens, ids, weights, gate_up, down, out, hess,
                  feats, shares, hid, part, got_ax, got_ay, got_bx, got_by, got_z,
                  w_gate, w_down, send_sem, recv_sem, load_sem):
     rows, width = tokens.shape
@@ -36,7 +36,6 @@
     at_end = z % (PLANES - 1) == 0
     inside = z % (PLANES - 1) != 0
     a1, a2, a3 = pick(FIRST, z), pick(SECOND, z), pick(THIRD, z)
-    order = (z, a1, a3, a2)
     lo, hi = pl.ds(0, half), pl.ds(half, half)
     all_rows = pl.ds(0, rows)
     started = []
@@ -104,15 +103,24 @@
         for q, name in ((j, "c0"), (xj, "c1"), (yj, "c2"), (dj, "c3")):
             landed(feats.at[1 - c, k, q], name, k)
 
+    def share_table():
+        lanes = shares.shape[-1]
+        share = weights[...] / jnp.sum(weights[...], axis=1, keepdims=True)
+        lane = lax.broadcasted_iota(jnp.int32, (rows, lanes), 1)
+        dense = jnp.zeros((rows, lanes), jnp.float32)
+        for q in range(ids.shape[1]):
+            dense = dense + jnp.where(ids[:, q:q + 1] == lane, share[:, q:q + 1], 0.0)
+        square = jnp.concatenate([dense, jnp.zeros((lanes - rows, lanes), jnp.float32)], axis=0)
+        shares[z, j] = square.T[:shares.shape[2]]
+
     def my_share(k):
         lanes = shares.shape[-1]
-        row, off = me * rows // lanes, me * rows % lanes
         lane = lax.broadcasted_iota(jnp.int32, (rows, lanes), 1)
         line = lax.broadcasted_iota(jnp.int32, (rows, lanes), 0)
         columns = []
         for q in range(PLANE):
-            values = jnp.broadcast_to(shares[k, q, pl.ds(row, 1), :], (rows, lanes))
-            columns.append(jnp.sum(jnp.where(lane == line + off, values, 0.0), axis=1, keepdims=True))
+            values = jnp.broadcast_to(shares[k, q, pl.ds(me, 1), :], (rows, lanes))
+            columns.append(jnp.sum(jnp.where(lane == line, values, 0.0), axis=1, keepdims=True))
         return jnp.concatenate(columns, axis=0)
 
     def up_side(k, w):
@@ -168,40 +176,53 @@
         landed(got_by.at[k, lo], "by0", k)
         landed(got_by.at[k, hi], "by1", k)
 
-    def z_sem(slot, k):
-        return recv_sem.at[(NAMES.index("z0") + slot) * PLANES + k]
-
-    def z_copy(k):
+    pieces = [slice(0, width // 2), slice(width // 2, width)]
+
+    def z_sem(slot, k, p):
+        return recv_sem.at[(NAMES.index("z00") + 2 * slot + p) * PLANES + k]
+
+    def z_copies(k, when):
         slot = jnp.where(k > z, 0, 1)
         to = jnp.where(k > z, me + PLANE, me - PLANE)
-        copy = pltpu.make_async_remote_copy(
-            src_ref=part.at[k, j], dst_ref=got_z.at[slot, k], send_sem=send_sem.at[len(started)],
-            recv_sem=z_sem(slot, k), device_id=(to, c), device_id_type=pl.DeviceIdType.MESH)
-        return copy, slot
+        copies = []
+        for p, cols in enumerate(pieces):
+            copy = pltpu.make_async_remote_copy(
+                src_ref=part.at[k, j, :, cols], dst_ref=got_z.at[slot, k, :, cols],
+                send_sem=send_sem.at[len(started)], recv_sem=z_sem(slot, k, p),
+                device_id=(to, c), device_id_type=pl.DeviceIdType.MESH)
+            started.append((copy, when))
+            copies.append(copy)
+        return copies, slot
+
+    def z_landed(slot, k, p):
+        dst = got_z.at[slot, k, :, pieces[p]]
+        pltpu.make_async_remote_copy(
+            src_ref=dst, dst_ref=dst, send_sem=send_sem.at[0], recv_sem=z_sem(slot, k, p),
+            device_id=(me, 1 - c), device_id_type=pl.DeviceIdType.MESH).wait_recv()
 
     def chain_end(k):
-        copy, _ = z_copy(k)
-        started.append((copy, at_end))
+        copies, _ = z_copies(k, at_end)
 
         @pl.when(at_end)
         def _():
             plane_done(k)
-            part[k, j] = add_up(part[k, j], got_bx[k], got_by[k])
-            copy.start()
+            for copy, cols in zip(copies, pieces):
+                part[k, j, :, cols] = add_up(part[k, j, :, cols], got_bx[k, :, cols], got_by[k, :, cols])
+                copy.start()
 
     def chain_inside(k):
-        copy, slot = z_copy(k)
-        started.append((copy, inside))
+        copies, slot = z_copies(k, inside)
 
         @pl.when(inside)
         def _():
             plane_done(k)
-            copy.wait_recv()
-            part[k, j] = add_up(part[k, j], got_bx[k], got_by[k], got_z[slot, k])
-            copy.start()
+            for p, cols in enumerate(pieces):
+                z_landed(slot, k, p)
+                part[k, j, :, cols] = add_up(part[k, j, :, cols], got_bx[k, :, cols], got_by[k, :, cols],
+                                             got_z[slot, k, :, cols])
+                copies[p].start()
 
     feats[c, z, j] = tokens[...]
-    shares[z, j] = table[...]
     barrier = pltpu.get_barrier_semaphore()
 
     def greet(to, core):
@@ -216,43 +237,67 @@
     pl.when(inside)(lambda: pl.semaphore_wait(barrier, 5))
 
     for to, when in ((me - PLANE, z > 0), (me + PLANE, z < PLANES - 1)):
+        send(block(z, j), block(z, j), to, "zr", z, when=when)
+    send(block(z, j), block(z, j), ex, "xr", z)
+    send(block(z, j), block(z, j), ey, "yr", z)
+    across(z, j, "c0")
+    share_table()
+    for to, when in ((me - PLANE, z > 0), (me + PLANE, z < PLANES - 1)):
         send(shares.at[z, j], shares.at[z, j], to, "tz", z, when=when)
-        send(block(z, j), block(z, j), to, "zr", z, when=when)
-    sides(z)
-    across(z, j, "c0")
+    send(shares.at[z, j], shares.at[z, j], ex, "tx", z)
+    send(shares.at[z, j], shares.at[z, j], ey, "ty", z)
     column(a1)
     sides(a1)
-    relay(order[0])
+    relay(z)
     column(a2)
-    corner(order[0])
-    relay(order[1])
+    corner(z)
+    relay(a1)
     column(a3)
     sides(a3)
     sides(a2)
 
     load_gate.wait()
     load_down.wait()
-    count = None
-    for i, k in enumerate(order):
+
+    def up_round(k):
         other_core(k)
         w = my_share(k)
-        hits = jnp.sum((w > 0).astype(jnp.float32), axis=0, keepdims=True)
-        count = hits if count is None else count + hits
         up_side(k, w)
-        if i + 2 < PLANES:
-            relay(order[i + 2])
-        down_side(k, w, i == 0)
-        give(k)
-        if i + 1 < PLANES:
-            corner(order[i + 1])
-        if i >= 1:
-            pass_on(order[i - 1])
-        if i >= 2:
-            chain_end(order[i - 1])
-    pass_on(order[3])
+        return w, jnp.sum((w > 0).astype(jnp.float32), axis=0, keepdims=True)
+
+    w, count = up_round(z)
+    corner(a1)
+    down_side(z, w, True)
+    relay(a3)
+
+    w, hits = up_round(a1)
+    count = count + hits
+    relay(a2)
+    down_side(a1, w, False)
+    give(a1)
+    corner(a3)
+
+    w, hits = up_round(a3)
+    count = count + hits
+    corner(a2)
+    down_side(a3, w, False)
+    give(a3)
+    pass_on(a1)
+
+    w, hits = up_round(a2)
+    count = count + hits
+    down_side(a2, w, False)
+    give(a2)
+
+    pass_on(a3)
+    chain_end(a1)
+    pass_on(a2)
+    give(z)
     hess[0] = hess[0] * (2.0 / count)
-    chain_end(order[3])
+    chain_end(a3)
     chain_inside(a3)
+    pass_on(z)
+    chain_end(a2)
     chain_inside(pick((0, 0, 3, 0), z))
     chain_inside(pick((0, 2, 1, 0), z))
     plane_done(z)
@@ -260,17 +305,18 @@
     @pl.when(at_end)
     def _():
         slot = jnp.where(z > 0, 0, 1)
-        pltpu.make_async_remote_copy(
-            src_ref=part.at[z, j], dst_ref=got_z.at[slot, z], send_sem=send_sem.at[0],
-            recv_sem=z_sem(slot, z), device_id=(me, 1 - c),
-            device_id_type=pl.DeviceIdType.MESH).wait_recv()
-        out[...] = add_up(part[z, j], got_bx[z], got_by[z], got_z[slot, z])
+        for p, cols in enumerate(pieces):
+            z_landed(slot, z, p)
+            out[:, cols] = add_up(part[z, j, :, cols], got_bx[z, :, cols], got_by[z, :, cols],
+                                  got_z[slot, z, :, cols])
 
     @pl.when(inside)
     def _():
-        landed(got_z.at[0, z], "z0", z)
-        landed(got_z.at[1, z], "z1", z)
-        out[...] = add_up(part[z, j], got_bx[z], got_by[z], got_z[0, z], got_z[1, z])
+        for p, cols in enumerate(pieces):
+            z_landed(0, z, p)
+            z_landed(1, z, p)
+            out[:, cols] = add_up(part[z, j, :, cols], got_bx[z, :, cols], got_by[z, :, cols],
+                                  got_z[0, z, :, cols], got_z[1, z, :, cols])
 
     for copy, when in started:
         if when is None:
@@ -284,9 +330,6 @@
     experts = lax.axis_size("expert")
     units = gate_up.shape[2]
     lanes = 128
-    share = route_weights / jnp.sum(route_weights, axis=1, keepdims=True)
-    hit = route_ids[None] == jnp.arange(experts, dtype=jnp.int32)[:, None, None]
-    table = jnp.sum(jnp.where(hit, share[None], 0.0), axis=2).reshape(experts * rows // lanes, lanes)
     bf, f32 = jnp.bfloat16, jnp.float32
     out, hess = pl.pallas_call(
         layer_kernel,
@@ -294,11 +337,11 @@
             jax.ShapeDtypeStruct((rows, width), bf),
             jax.ShapeDtypeStruct((1, units, 2 * units), f32),
         ),
-        in_specs=[pl.BlockSpec(memory_space=pltpu.VMEM)] * 2 + [pl.BlockSpec(memory_space=pl.ANY)] * 2,
+        in_specs=[pl.BlockSpec(memory_space=pltpu.VMEM)] * 3 + [pl.BlockSpec(memory_space=pl.ANY)] * 2,
         out_specs=(pl.BlockSpec(memory_space=pltpu.VMEM),) * 2,
         scratch_shapes=[
             pltpu.VMEM((2, PLANES, PLANE, rows, width), bf),
-            pltpu.VMEM((PLANES, PLANE) + table.shape, f32),
+            pltpu.VMEM((PLANES, PLANE, experts, lanes), f32),
             pltpu.VMEM((2, PLANES, PLANE * rows, units), bf),
             pltpu.VMEM((PLANES, PLANE, rows, width), bf),
             pltpu.VMEM((PLANES, rows // 2, width), bf),
@@ -316,7 +359,7 @@
             collective_id=0, has_side_effects=True, vmem_limit_bytes=56 * 1024 * 1024
         ),
         name="moe_layer",
-    )(tokens, table, gate_up, down_proj)
+    )(tokens, route_ids, route_weights, gate_up, down_proj)
     return (out, hess)
 
 

time: 115 us -> 96.4 us (0.84); the launches traced: 114 us -> 96.1 us
  Pallas kernels: 106 us -> 88.7 us
  other arithmetic: 2.11 us -> 0 us
  local copies, waits for them, and re-layouts: 4.69 us -> 6.8 us
    pallas_call x1, Pallas kernels: 106 us -> 88.7 us  [kernel_body(): pl.pallas_call(layer_kernel, out_shape=(jax.ShapeDtypeStruct((rows, width...]
    unnamed x2 -> x4, local copies, waits for them, and re-layouts: 4.03 us -> 6.8 us
    reduce_sum x2 -> x0, other arithmetic: 1.42 us -> none  [the longest x1 0.72 us: kernel_body(): jnp.sum(jnp.where(hit, share[None], 0.0), axis=2)]
where the time goes in v3:
time: 96.4 us; the launch traced here: 96.1 us
  Pallas kernels  88.7 us (92%)
  local copies, waits for them, and re-layouts  6.8 us (7%)
    pallas_call x1, Pallas kernels, kernel_body(): pl.pallas_call(layer_kernel, out_shape=(jax.ShapeDtypeStruct((rows, width...  88.7 us
    unnamed x4, local copies, waits for them, and re-layouts  6.8 us

profile of v3, /device:TPU:8, one launch (start us, length us, event | category | flops | bytes accessed | tf_op | source)
XLA Modules:
  0.0 96.1 jit_solution(11348198494594082654)
XLA Ops:
  0.6 1.4 %copy.7.ids = s32[64,8]{1,0:T(8,128)} copy(s32[64,8]{0,1:T(8,128)} %param.6) | data formatting | bytes 4096 | tf_op args[1]
  2.0 1.4 %copy.8.weights = f32[64,8]{1,0:T(8,128)} copy(f32[64,8]{0,1:T(8,128)} %param.7) | data formatting | bytes 4096 | tf_op args[2]
  3.4 88.7 %moe_layer.1 = (bf16[64,2048]{1,0:T(8,128)(2,1)}, f32[1,384,768]{2,1,0:T(8,128)}) custom-call(bf16[64,2048]{1,0:T(8,128)(2,1)} %tokens.1, s32[64,8]{1,0:T(8,128)} %copy.7.ids, f32[64,8]{1,0:T(8,128)} %copy.8.weights, bf16[1,2,384,4096]{3,2,1,0:T(8,128)(2,1)} %gate_up.1, bf16[1,768,2048]{2,1,0:T(8,128)(2,1)} %down.1), custom_call_target="tpu_custom_call" | custom-call | tf_op jit(solution)/shard_map/moe_layer/pallas_call | solution.py:334
  92.1 1.7 %copy.11 = bf16[64,2048]{1,0:T(8,128)(2,1)} copy(bf16[64,2048]{1,0:T(8,128)(2,1)} %get-tuple-element.4) | data formatting | bytes 524288
  93.8 2.4 %copy.12 = f32[1,384,768]{2,1,0:T(8,128)} copy(f32[1,384,768]{2,1,0:T(8,128)} %get-tuple-element.5) | data formatting | bytes 2359296

commit v4 on v3

--- a/solution.py
+++ b/solution.py
@@ -22,9 +22,9 @@
     return chosen
 
 
-def layer_kernel(tokens, ids, weights, gate_up, down, out, hess,
+def layer_kernel(tokens, ids, weights, gate_up, down, out, hess_out,
                  feats, shares, hid, part, got_ax, got_ay, got_bx, got_by, got_z,
-                 w_gate, w_down, send_sem, recv_sem, load_sem):
+                 w_gate, w_down, hess, send_sem, recv_sem, load_sem):
     rows, width = tokens.shape
     half = rows // 2
     units = hid.shape[-1]
@@ -104,14 +104,13 @@
             landed(feats.at[1 - c, k, q], name, k)
 
     def share_table():
-        lanes = shares.shape[-1]
-        share = weights[...] / jnp.sum(weights[...], axis=1, keepdims=True)
-        lane = lax.broadcasted_iota(jnp.int32, (rows, lanes), 1)
-        dense = jnp.zeros((rows, lanes), jnp.float32)
-        for q in range(ids.shape[1]):
-            dense = dense + jnp.where(ids[:, q:q + 1] == lane, share[:, q:q + 1], 0.0)
-        square = jnp.concatenate([dense, jnp.zeros((lanes - rows, lanes), jnp.float32)], axis=0)
-        shares[z, j] = square.T[:shares.shape[2]]
+        experts, lanes = shares.shape[2:]
+        share = weights[...] / jnp.sum(weights[...], axis=0, keepdims=True)
+        expert = lax.broadcasted_iota(jnp.int32, (experts, rows), 0)
+        dense = jnp.zeros((experts, rows), jnp.float32)
+        for q in range(ids.shape[0]):
+            dense = dense + jnp.where(ids[q:q + 1, :] == expert, share[q:q + 1, :], 0.0)
+        shares[z, j] = jnp.concatenate([dense, jnp.zeros((experts, lanes - rows), jnp.float32)], axis=1)
 
     def my_share(k):
         lanes = shares.shape[-1]
@@ -142,7 +141,7 @@
             cols = slice(side * units, (side + 1) * units)
             gram = lax.dot_general(mine, hid[side, k], (((0,), (0,)), ((), ())),
                                    preferred_element_type=jnp.float32)
-            hess[0, :, cols] = gram if first else hess[0, :, cols] + gram
+            hess[:, cols] = gram if first else hess[:, cols] + gram
         step = 512
         for start in range(0, width, step):
             cols = slice(start, start + step)
@@ -293,7 +292,9 @@
     chain_end(a1)
     pass_on(a2)
     give(z)
-    hess[0] = hess[0] * (2.0 / count)
+    hess[...] = hess[...] * (2.0 / count)
+    store = pltpu.make_async_copy(hess, hess_out.at[0], load_sem.at[2])
+    store.start()
     chain_end(a3)
     chain_inside(a3)
     pass_on(z)
@@ -318,11 +319,20 @@
             out[:, cols] = add_up(part[z, j, :, cols], got_bx[z, :, cols], got_by[z, :, cols],
                                   got_z[0, z, :, cols], got_z[1, z, :, cols])
 
+    store.wait()
     for copy, when in started:
         if when is None:
             copy.wait_send()
         else:
             pl.when(when)(copy.wait_send)
+
+
+def results_kernel(out_in, hess_in, out, hess, sem):
+    copies = [pltpu.make_async_copy(out_in, out, sem.at[0]), pltpu.make_async_copy(hess_in, hess, sem.at[1])]
+    for copy in copies:
+        copy.start()
+    for copy in copies:
+        copy.wait()
 
 
 def kernel_body(tokens, route_ids, route_weights, gate_up, down_proj):
@@ -338,7 +348,7 @@
             jax.ShapeDtypeStruct((1, units, 2 * units), f32),
         ),
         in_specs=[pl.BlockSpec(memory_space=pltpu.VMEM)] * 3 + [pl.BlockSpec(memory_space=pl.ANY)] * 2,
-        out_specs=(pl.BlockSpec(memory_space=pltpu.VMEM),) * 2,
+        out_specs=(pl.BlockSpec(memory_space=pltpu.VMEM), pl.BlockSpec(memory_space=pl.ANY)),
         scratch_shapes=[
             pltpu.VMEM((2, PLANES, PLANE, rows, width), bf),
             pltpu.VMEM((PLANES, PLANE, experts, lanes), f32),
@@ -351,16 +361,25 @@
             pltpu.VMEM((2, PLANES, rows, width), bf),
             pltpu.VMEM(gate_up.shape[1:], bf),
             pltpu.VMEM(down_proj.shape[1:], bf),
+            pltpu.VMEM((units, 2 * units), f32),
             pltpu.SemaphoreType.DMA((SENDS,)),
             pltpu.SemaphoreType.DMA((len(NAMES) * PLANES,)),
-            pltpu.SemaphoreType.DMA((2,)),
+            pltpu.SemaphoreType.DMA((3,)),
         ],
         compiler_params=pltpu.CompilerParams(
             collective_id=0, has_side_effects=True, vmem_limit_bytes=56 * 1024 * 1024
         ),
         name="moe_layer",
-    )(tokens, route_ids, route_weights, gate_up, down_proj)
-    return (out, hess)
+    )(tokens, route_ids.T, route_weights.T, gate_up, down_proj)
+    return pl.pallas_call(
+        results_kernel,
+        out_shape=(jax.ShapeDtypeStruct(out.shape, out.dtype), jax.ShapeDtypeStruct(hess.shape, hess.dtype)),
+        in_specs=[pl.BlockSpec(memory_space=pl.ANY)] * 2,
+        out_specs=(pl.BlockSpec(memory_space=pl.ANY),) * 2,
+        scratch_shapes=[pltpu.SemaphoreType.DMA((2,))],
+        compiler_params=pltpu.CompilerParams(vmem_limit_bytes=56 * 1024 * 1024),
+        name="results",
+    )(out, hess)
 
 
 def body(tokens, route_ids, route_weights, gate_up, down_proj):

time: 96.4 us -> 134 us (1.39)
  Pallas kernels: 88.7 us -> 133 us
  local copies, waits for them, and re-layouts: 6.8 us -> 0 us
    pallas_call x0 -> x1, Pallas kernels: none -> 44.8 us  [kernel_body(): pl.pallas_call(results_kernel, out_shape=(jax.ShapeDtypeStruct(out.shape,...]
    unnamed x4 -> x0, local copies, waits for them, and re-layouts: 6.8 us -> none
where the time goes in v4:
time: 134 us
  Pallas kernels  133 us (99%)
    pallas_call x1, Pallas kernels, kernel_body(): pl.pallas_call(layer_kernel, out_shape=(jax.ShapeDtypeStruct((rows, width...  88.7 us
    pallas_call x1, Pallas kernels, kernel_body(): pl.pallas_call(results_kernel, out_shape=(jax.ShapeDtypeStruct(out.shape,...  44.8 us

profile of v4, /device:TPU:8, one launch (start us, length us, event | category | flops | bytes accessed | tf_op | source)
XLA Modules:
  0.0 134.1 jit_solution(1657542551203649613)
XLA Ops:
  0.6 88.7 %moe_layer.1 = (bf16[64,2048]{1,0:T(8,128)(2,1)}, f32[1,384,768]{2,1,0:T(8,128)}) custom-call(bf16[64,2048]{1,0:T(8,128)(2,1)} %tokens.1, s32[8,64]{1,0:T(8,128)} %bitcast.2, f32[8,64]{1,0:T(8,128)} %bitcast.3, bf16[1,2,384,4096]{3,2,1,0:T(8,128)(2,1)} %gate_up.1, bf16[1,768,2048]{2,1,0:T(8,128)(2,1)} %down.1), custom_call_target="tpu_custom_call" | custom-call | tf_op jit(solution)/shard_map/moe_layer/pallas_call | solution.py:344
  89.3 44.8 %results.1 = (bf16[64,2048]{1,0:T(8,128)(2,1)}, f32[1,384,768]{2,1,0:T(8,128)}) custom-call(bf16[64,2048]{1,0:T(8,128)(2,1)} %get-tuple-element.4.out_in, f32[1,384,768]{2,1,0:T(8,128)} %get-tuple-element.5.hess_in), custom_call_target="tpu_custom_call" | custom-call | tf_op jit(solution)/shard_map/results/pallas_call | solution.py:374

commit v5 on v4

--- a/solution.py
+++ b/solution.py
@@ -10,7 +10,7 @@
 FIRST = (1, 2, 1, 2)
 SECOND = (2, 0, 3, 1)
 THIRD = (3, 3, 0, 0)
-NAMES = ("zr", "xr", "yr", "dx", "dy", "c0", "c1", "c2", "c3", "tz", "tx", "ty", "td", "hr",
+NAMES = ("zd", "zr", "xr", "yr", "dx", "dy", "c0", "c1", "c2", "c3", "tz", "tx", "ty", "td", "hr",
          "ax", "ay", "bx0", "bx1", "by0", "by1", "z00", "z01", "z10", "z11")
 SENDS = 128
 
@@ -82,21 +82,46 @@
         send(block(k, j), block(k, j), to, "zr", k, when=inside)
         across(k, j, "c0")
 
-    def relay(k):
+    def relay(k, halves, when=None):
         landed(shares.at[k, yj], "ty", k)
         landed(shares.at[k, xj], "tx", k)
         send(shares.at[k, yj], shares.at[k, yj], ex, "td", k)
         landed(block(k, yj), "yr", k)
-        send(block(k, yj, lo), block(k, yj, lo), ex, "dx", k)
+        if halves:
+            send(block(k, yj, lo), block(k, yj, lo), ex, "dx", k, when=when)
         across(k, yj, "c2")
         landed(block(k, xj), "xr", k)
-        send(block(k, xj, hi), block(k, xj, hi), ey, "dy", k)
+        if halves:
+            send(block(k, xj, hi), block(k, xj, hi), ey, "dy", k, when=when)
         across(k, xj, "c1")
 
-    def corner(k):
+    def corner_own():
+        landed(shares.at[z, dj], "td", z)
+        landed(block(z, dj, lo), "dx", z)
+        landed(block(z, dj, hi), "dy", z)
+        for to, when in ((me - PLANE, z > 0), (me + PLANE, z < PLANES - 1)):
+            send(block(z, dj), block(z, dj), to, "zd", z, when=when)
+        across(z, dj, "c3")
+
+    def corner_near(k):
         landed(shares.at[k, dj], "td", k)
-        landed(block(k, dj, lo), "dx", k)
-        landed(block(k, dj, hi), "dy", k)
+        landed(block(k, dj), "zd", k)
+        to = jnp.where(k < z, me + PLANE, me - PLANE)
+        send(block(k, dj), block(k, dj), to, "zd", k, when=inside)
+        across(k, dj, "c3")
+
+    def corner_far(k):
+        landed(shares.at[k, dj], "td", k)
+
+        @pl.when(at_end)
+        def _():
+            landed(block(k, dj, lo), "dx", k)
+            landed(block(k, dj, hi), "dy", k)
+
+        @pl.when(inside)
+        def _():
+            landed(block(k, dj), "zd", k)
+
         across(k, dj, "c3")
 
     def other_core(k):
@@ -221,7 +246,6 @@
                                              got_z[slot, k, :, cols])
                 copies[p].start()
 
-    feats[c, z, j] = tokens[...]
     barrier = pltpu.get_barrier_semaphore()
 
     def greet(to, core):
@@ -232,6 +256,7 @@
     greet(ey, c)
     pl.when(z > 0)(lambda: greet(me - PLANE, c))
     pl.when(z < PLANES - 1)(lambda: greet(me + PLANE, c))
+    feats[c, z, j] = tokens[...]
     pl.when(at_end)(lambda: pl.semaphore_wait(barrier, 4))
     pl.when(inside)(lambda: pl.semaphore_wait(barrier, 5))
 
@@ -247,10 +272,10 @@
     send(shares.at[z, j], shares.at[z, j], ey, "ty", z)
     column(a1)
     sides(a1)
-    relay(z)
+    relay(z, True)
     column(a2)
-    corner(z)
-    relay(a1)
+    corner_own()
+    relay(a1, False)
     column(a3)
     sides(a3)
     sides(a2)
@@ -265,20 +290,20 @@
         return w, jnp.sum((w > 0).astype(jnp.float32), axis=0, keepdims=True)
 
     w, count = up_round(z)
-    corner(a1)
+    corner_near(a1)
     down_side(z, w, True)
-    relay(a3)
+    relay(a3, True, when=at_end)
 
     w, hits = up_round(a1)
     count = count + hits
-    relay(a2)
+    relay(a2, False)
+    corner_near(a2)
     down_side(a1, w, False)
     give(a1)
-    corner(a3)
+    corner_far(a3)
 
     w, hits = up_round(a3)
     count = count + hits
-    corner(a2)
     down_side(a3, w, False)
     give(a3)
     pass_on(a1)
@@ -327,12 +352,17 @@
             pl.when(when)(copy.wait_send)
 
 
-def results_kernel(out_in, hess_in, out, hess, sem):
-    copies = [pltpu.make_async_copy(out_in, out, sem.at[0]), pltpu.make_async_copy(hess_in, hess, sem.at[1])]
-    for copy in copies:
-        copy.start()
-    for copy in copies:
-        copy.wait()
+def results_kernel(out_in, hess_in, out, hess, out_held, hess_held, in_sem, out_sem):
+    pairs = ((hess_in, hess_held, hess), (out_in, out_held, out))
+    loads = [pltpu.make_async_copy(src, held, in_sem.at[n]) for n, (src, held, _) in enumerate(pairs)]
+    stores = [pltpu.make_async_copy(held, dst, out_sem.at[n]) for n, (_, held, dst) in enumerate(pairs)]
+    for load in loads:
+        load.start()
+    for load, store in zip(loads, stores):
+        load.wait()
+        store.start()
+    for store in stores:
+        store.wait()
 
 
 def kernel_body(tokens, route_ids, route_weights, gate_up, down_proj):
@@ -376,7 +406,8 @@
         out_shape=(jax.ShapeDtypeStruct(out.shape, out.dtype), jax.ShapeDtypeStruct(hess.shape, hess.dtype)),
         in_specs=[pl.BlockSpec(memory_space=pl.ANY)] * 2,
         out_specs=(pl.BlockSpec(memory_space=pl.ANY),) * 2,
-        scratch_shapes=[pltpu.SemaphoreType.DMA((2,))],
+        scratch_shapes=[pltpu.VMEM(out.shape, out.dtype), pltpu.VMEM(hess.shape, hess.dtype),
+                        pltpu.SemaphoreType.DMA((2,)), pltpu.SemaphoreType.DMA((2,))],
         compiler_params=pltpu.CompilerParams(vmem_limit_bytes=56 * 1024 * 1024),
         name="results",
     )(out, hess)

time: 134 us -> 97.6 us (0.73)
  Pallas kernels: 133 us -> 96.8 us
    pallas_call x1, Pallas kernels: 44.8 us -> 2.4 us  [kernel_body(): pl.pallas_call(results_kernel, out_shape=(jax.ShapeDtypeStruct(out.shape,...]
    pallas_call x1, Pallas kernels: 88.7 us -> 94.4 us  [kernel_body(): pl.pallas_call(layer_kernel, out_shape=(jax.ShapeDtypeStruct((rows, width...]
where the time goes in v5:
time: 97.6 us; the launch traced here: 97.4 us
  Pallas kernels  96.8 us (99%)
    pallas_call x1, Pallas kernels, kernel_body(): pl.pallas_call(layer_kernel, out_shape=(jax.ShapeDtypeStruct((rows, width...  94.4 us
    pallas_call x1, Pallas kernels, kernel_body(): pl.pallas_call(results_kernel, out_shape=(jax.ShapeDtypeStruct(out.shape,...  2.4 us

profile of v5, /device:TPU:8, one launch (start us, length us, event | category | flops | bytes accessed | tf_op | source)
XLA Modules:
  0.0 97.4 jit_solution(9091079723317083982)
XLA Ops:
  0.6 94.4 %moe_layer.1 = (bf16[64,2048]{1,0:T(8,128)(2,1)}, f32[1,384,768]{2,1,0:T(8,128)}) custom-call(bf16[64,2048]{1,0:T(8,128)(2,1)} %tokens.1, s32[8,64]{1,0:T(8,128)} %bitcast.2, f32[8,64]{1,0:T(8,128)} %bitcast.3, bf16[1,2,384,4096]{3,2,1,0:T(8,128)(2,1)} %gate_up.1, bf16[1,768,2048]{2,1,0:T(8,128)(2,1)} %down.1), custom_call_target="tpu_custom_call" | custom-call | tf_op jit(solution)/shard_map/moe_layer/pallas_call | solution.py:374
  95.0 2.4 %results.1 = (bf16[64,2048]{1,0:T(8,128)(2,1)}, f32[1,384,768]{2,1,0:T(8,128)}) custom-call(bf16[64,2048]{1,0:T(8,128)(2,1)} %get-tuple-element.4.out_in, f32[1,384,768]{2,1,0:T(8,128)} %get-tuple-element.5.hess_in), custom_call_target="tpu_custom_call" | custom-call | tf_op jit(solution)/shard_map/results/pallas_call | solution.py:404
